TPU v7x, 256 devices: a whole 4x4x8 slice. The times are simulated.
256 devices in a mesh: dp: 64 (over x, z, y_lo), tensor: 4 (over y_hi, core).
Axes of the slice: x: 4, y: 4 (y_hi: 2, y_lo: 2; y = y_hi * 2 + y_lo), z: 8, core: 2. Of those that a mesh axis runs over, the one named last changes fastest.
Arguments:
- tokens: bfloat16 [32768, 8192], P(('dp', 'tensor')), may hold values from -6 to 6
- gate_pre: bfloat16 [32768, 1024], P('dp', 'tensor'), may hold values from -6 to 6
- up_pre: bfloat16 [32768, 1024], P('dp', 'tensor'), may hold values from -6 to 6
- d_hidden: bfloat16 [32768, 1024], P('dp', 'tensor'), may hold values from -0.032958984 to 0.032958984
- left_roots: bfloat16 [1024, 8, 2, 1024], P('dp'), as said below
- right_roots: bfloat16 [2, 1024, 1024], P(None, 'tensor'), as said below
Outputs:
- update: float32 [1024, 8, 2, 1024], P('dp', None, None, 'tensor')
Inputs may be any that keep to these rules, and one draw needn't show every extreme that they name: Every block is symmetric: left_roots[r, b, m, k] equals left_roots[k, b, m, r], and right_roots[m, j, c] equals right_roots[m, c, j]; each block is positive definite. Each right_roots[m] is symmetric and positive definite.
All inputs are finite; a program needn't handle non-finite values.
Results may differ from a plain program's by a relative error of at most 0.005.
Values may be sent and summed in bfloat16 or wider, within the bound.
A program may use at most 128 MiB of HBM per device.

v0:
```python
import jax
import jax.numpy as jnp
from jax import lax
from jax.sharding import PartitionSpec as P


def precondition(grad, left_part, right_part):
    grad_low = grad.astype(jnp.bfloat16)
    partial_mix = jnp.einsum(
        "rbmj,mjc->rbmc", grad_low, right_part, preferred_element_type=jnp.float32
    )
    mixed = lax.psum_scatter(partial_mix, "tensor", scatter_dimension=3, tiled=True)
    mixed_low = mixed.astype(jnp.bfloat16)
    whole_block = lax.all_gather(mixed_low, "dp", axis=0, tiled=True)
    return jnp.einsum("rbmk,kbmc->rbmc", left_part, whole_block, preferred_element_type=jnp.float32)


def local(tokens, gate_pre, up_pre, d_hidden, left_roots, right_roots):
    gate_val = gate_pre.astype(jnp.float32)
    up_val = up_pre.astype(jnp.float32)
    cotangent = d_hidden.astype(jnp.float32)
    sig_gate = jax.nn.sigmoid(gate_val)
    d_gate = (cotangent * up_val * sig_gate * (1.0 + gate_val * (1.0 - sig_gate))).astype(
        jnp.bfloat16
    )
    d_up = (cotangent * gate_val * sig_gate).astype(jnp.bfloat16)
    group_rows = lax.all_gather(tokens, "tensor", axis=0, tiled=True)
    num_blocks = left_roots.shape[1]
    block_size = left_roots.shape[3]
    owned = left_roots.shape[0]
    hidden_local = d_gate.shape[1]
    blocked = group_rows.reshape(group_rows.shape[0], num_blocks, block_size)
    stacked = jnp.concatenate([d_gate, d_up], axis=1)
    grad = lax.psum_scatter(
        jnp.einsum("tbr,tn->rbn", blocked, stacked, preferred_element_type=jnp.float32),
        "dp",
        scatter_dimension=0,
        tiled=True,
    )
    grad = grad.reshape(owned, num_blocks, 2, hidden_local)
    return precondition(grad, left_roots, right_roots)


def solution(mesh):
    in_specs = (
        P(("dp", "tensor"), None),
        P("dp", "tensor"),
        P("dp", "tensor"),
        P("dp", "tensor"),
        P("dp", None, None, None),
        P(None, "tensor", None),
    )
    out_specs = P("dp", None, None, "tensor")
    return jax.shard_map(local, mesh=mesh, in_specs=in_specs, out_specs=out_specs, check_vma=False)
```

profile of v0, /device:TPU:16, one launch (start us, length us, event | category | flops | bytes accessed | tf_op | source)
XLA Modules:
  0.0 844.5 jit_solution(9615186797505770220)
XLA Ops:
  6.5 0.0 copy-start
  6.5 0.0 all-gather.3.cloned.1.call-start
  6.5 4.2 copy.22
  10.7 0.0 all-gather.3.cloned.1.call-update
  10.7 0.0 reduce-scatter.3.cloned.1.call-start
  10.8 1.1 copy.21
  11.9 1.1 copy.20
  13.0 1.1 copy.19
  14.1 0.3 fusion.3
  14.4 62.6 %all-gather.3.cloned.1.call-done = bf16[512,8192]{0,1:T(8,128)(2,1)} async-done(((bf16[128,8192]{0,1:T(8,128)(2,1)}), bf16[512,8192]{0,1:T(8,128)(2,1)}) %all-gather.3.cloned.1.call-update) | async-done | bytes 8388624 | tf_op jit(solution)/shard_map/all_gather | solution.py:27
  76.9 11.7 %convolution_bitcast_fusion = f32[1024,8,512]{0,2,1:T(8,128)} fusion(bf16[512,8,1024]{0,2,1:T(8,128)(2,1)} %bitcast.16, bf16[512,256]{0,1:T(8,128)(2,1)S(1)} %get-tuple-element.6, bf16[512,256]{0,1:T(8,128)(2,1)S(1)} %get-tuple-element.5), kind=kOutput, calls=%fused_computation | convolution fusion | flops 4296015872 | bytes 25690112 | tf_op jit(solution)/shard_map/tbr,tn->rbn/dot_general | solution.py:35
  88.6 17.6 %copy.24 = f32[1024,8,512]{2,1,0:T(8,128)} copy(f32[1024,8,512]{0,2,1:T(8,128)} %convolution_bitcast_fusion) | data formatting | bytes 33554432 | tf_op jit(solution)/shard_map/tbr,tn->rbn/transpose | solution.py:35
  106.2 0.0 copy-start.1
  106.2 0.0 reduce-scatter.3.cloned.1.call-update
  106.2 0.0 reduce-scatter.5.cloned.1.call-start
  106.3 374.0 %reduce-scatter.3.cloned.1.call-done = f32[16,8,512]{2,1,0:T(8,128)} async-done(((f32[1024,8,512]{2,1,0:T(8,128)}), f32[16,8,512]{2,1,0:T(8,128)}) %reduce-scatter.3.cloned.1.call-update) | async-done | bytes 262160 | tf_op jit(solution)/shard_map/reduce_scatter | solution.py:34
  480.3 1.0 convert_element_type.29
  481.2 0.0 copy-done
  481.2 1.3 convolution_bitcast_fusion.1
  482.5 0.0 reduce-scatter.5.cloned.1.call-update
  482.6 0.0 all-gather.5.cloned.1.call-start
  482.6 32.3 %reduce-scatter.5.cloned.1.call-done = f32[16,8,2,256]{3,0,2,1:T(8,128)} async-done(((f32[16,8,2,1024]{3,0,2,1:T(8,128)}), f32[16,8,2,256]{3,0,2,1:T(8,128)}) %reduce-scatter.5.cloned.1.call-update) | async-done | bytes 262160 | tf_op jit(solution)/shard_map/reduce_scatter | solution.py:12
  514.9 1.6 convert_element_type.31
  516.5 0.0 all-gather.5.cloned.1.call-update
  516.5 315.9 %all-gather.5.cloned.1.call-done = bf16[1024,8,2,256]{3,0,2,1:T(8,128)(2,1)} async-done(((bf16[16,8,2,256]{3,0,2,1:T(8,128)(2,1)}), bf16[1024,8,2,256]{3,0,2,1:T(8,128)(2,1)}) %all-gather.5.cloned.1.call-update) | async-done | bytes 8388624 | tf_op jit(solution)/shard_map/all_gather | solution.py:14
  832.4 0.0 copy-done.1
  832.4 4.6 convolution_bitcast_fusion.2
  837.0 0.9 copy.27
Async XLA Ops:
  6.5 474.7 %copy-start = (bf16[2,256,1024]{2,1,0:T(8,128)(2,1)S(1)}, bf16[2,256,1024]{2,1,0:T(8,128)(2,1)}, u32[]{:S(2)}) copy-start(bf16[2,256,1024]{2,1,0:T(8,128)(2,1)} %param.11) | copy-start | bytes 3145732
  6.5 70.4 %all-gather.3.cloned.1.call-start = ((), (), s32[]{:S(2)}) async-start(), calls=%async_computation.2 | async-start | bytes 10485760 | tf_op jit(solution)/shard_map/all_gather | solution.py:27
  10.7 469.6 %reduce-scatter.3.cloned.1.call-start = ((), (), s32[]{:S(2)}) async-start(), calls=%async_computation.3 | async-start | bytes 17039360 | tf_op jit(solution)/shard_map/reduce_scatter | solution.py:34
  106.2 726.2 %copy-start.1 = (bf16[16,8,2,1024]{3,2,1,0:T(2,128)(2,1)S(1)}, bf16[16,8,2,1024]{3,2,1,0:T(2,128)(2,1)}, u32[]{:S(2)}) copy-start(bf16[16,8,2,1024]{3,2,1,0:T(2,128)(2,1)} %param.10) | copy-start | bytes 1572868
  106.2 408.7 %reduce-scatter.5.cloned.1.call-start = ((), (), s32[]{:S(2)}) async-start(), calls=%async_computation.4 | async-start | bytes 1310720 | tf_op jit(solution)/shard_map/reduce_scatter | solution.py:12
  482.6 349.9 %all-gather.5.cloned.1.call-start = ((), (), s32[]{:S(2)}) async-start(), calls=%async_computation.5 | async-start | bytes 8519680 | tf_op jit(solution)/shard_map/all_gather | solution.py:14
Sparse Core Ops, SparseCore 0:
  10.8 66.0 all-gather.2
  106.3 373.8 reduce-scatter.2
  483.1 31.7 reduce-scatter.4
  516.7 315.6 all-gather.4
where the time goes:
time: 845 us; the launch traced here: 844 us
  waiting for transfers between devices  785 us (93%)
  local copies, waits for them, and re-layouts  25.9 us (3%)
  matrix products  17.5 us (2%)
  between operations  13.2 us (2%)
    reduce_scatter x1, waiting for transfers between devices, local(): lax.psum_scatter(jnp.einsum('tbr,tn->rbn', blocked, stacked, preferred_el...  374 us
    all_gather x1, waiting for transfers between devices, precondition(): whole_block = lax.all_gather(mixed_low, 'dp', axis=0, tiled=True)  316 us
    all_gather x1, waiting for transfers between devices, local(): group_rows = lax.all_gather(tokens, 'tensor', axis=0, tiled=True)  62.6 us
    reduce_scatter x1, waiting for transfers between devices, precondition(): lax.psum_scatter(partial_mix, 'tensor', scatter_dimension=3, tiled=True)  32.3 us
    transpose x1, local copies, waits for them, and re-layouts, local(): jnp.einsum('tbr,tn->rbn', blocked, stacked, preferred_element_type=jnp.fl...  17.6 us
  transfers between devices with their start and end apart: 4, of which 4 were waited for; matrix products, arithmetic and copies ran while one was open for 0% of the time, Pallas kernels for 0%

commit v1 on v0

v1 whole, which is shorter than its diff:
```python
import jax
import jax.numpy as jnp
from jax import lax
from jax.experimental import pallas as pl
from jax.experimental.pallas import tpu as pltpu
from jax.sharding import PartitionSpec as P

MESH = pl.DeviceIdType.MESH
F32 = jnp.float32
BF16 = jnp.bfloat16

NX, NY, NZ = 4, 4, 8
SIZES = (96, 160, 160, 96)
STARTS = tuple(sum(SIZES[:i]) for i in range(len(SIZES)))
CHUNKS = len(SIZES)
HALF = 512


def device(x, y, z, core):
    return ((x * NZ + z) * 2 + lax.rem(y, 2), lax.div(y, 2) * 2 + core)


def ring(value, step, size):
    return lax.rem(value + (step + size), size)


def lane_of(y, core):
    return pl.multiple_of(
        lax.rem(y, 2) * 512 + (lax.div(y, 2) * 2 + core) * 128, 128
    )


def kernel(
    tok_hbm, gate_hbm, up_hbm, dh_hbm, left_hbm, right_hbm, out_ref,
    tok_ref, gate_ref, up_ref, dh_ref, left_ref, dga, tt, tk, fw, part, a_s, a_r, b_s, b_r, z_s, z_r, g_full,
    l1, lb, lg_f, lg_s, xm, rm, out_s,
    dg_send, dg_recv, dx_send, dx_recv, tk_send, tk_recv, tf_send,
    fw_recv, a_send, a_recv, bb_send, bb_recv, zz_send, zz_recv,
    g_send, g_recv, l1_send, l1_recv, l3_send, l3_recv, r_send, r_recv,
    t1_send, t1_recv, t2_send, t2_recv, in_sem,
):
    dp = lax.axis_index("dp")
    tensor = lax.axis_index("tensor")
    y_lo = lax.rem(dp, 2)
    z = lax.rem(lax.div(dp, 2), NZ)
    x = lax.div(dp, 2 * NZ)
    y_hi = lax.div(tensor, 2)
    core = lax.rem(tensor, 2)
    y = y_hi * 2 + y_lo
    other = 1 - core
    xp, xm1, xo = ring(x, 1, NX), ring(x, -1, NX), ring(x, 2, NX)
    yp, ym, yo = ring(y, 1, NY), ring(y, -1, NY), ring(y, 2, NY)

    def send(src, dst, ssem, rsem, dev):
        pltpu.make_async_remote_copy(
            src_ref=src, dst_ref=dst, send_sem=ssem, recv_sem=rsem,
            device_id=dev, device_id_type=MESH,
        ).start()

    def send_or_copy(is_me, src, dst, ssem, rsem, dev):
        @pl.when(is_me)
        def _():
            pltpu.make_async_copy(src, dst, rsem).start()

        @pl.when(jnp.logical_not(is_me))
        def _():
            send(src, dst, ssem, rsem, dev)

    def arrived(dst, rsem):
        pltpu.make_async_remote_copy(
            src_ref=dst, dst_ref=dst, send_sem=rsem, recv_sem=rsem,
            device_id=device(x, y, z, other), device_id_type=MESH,
        ).wait_recv()

    def sent(src, ssem):
        pltpu.make_async_remote_copy(
            src_ref=src, dst_ref=src, send_sem=ssem, recv_sem=ssem,
            device_id=device(x, y, z, other), device_id_type=MESH,
        ).wait_send()

    y_t = y_hi * 2 + core
    mine = lax.rem(x, 2)
    loads = [
        pltpu.make_async_copy(src, dst, in_sem.at[i])
        for i, (src, dst) in enumerate((
            (gate_hbm, gate_ref), (up_hbm, up_ref), (dh_hbm, dh_ref),
            (left_hbm.at[:, pl.ds(2 * y_t, 2)], left_ref), (tok_hbm, tok_ref),
            (right_hbm.at[mine], rm.at[tensor]),
        ))
    ]
    for load in loads:
        load.start()

    barrier = pltpu.get_barrier_semaphore()
    partners = []
    for step_x in range(NX):
        for step_y in range(NY):
            for cc in range(2):
                if step_x or step_y or cc:
                    partners.append(device(
                        ring(x, step_x, NX), ring(y, step_y, NY), z, lax.rem(core + cc, 2)
                    ))
    for step in range(1, NZ):
        partners.append(device(x, y, ring(z, step, NZ), core))
    for partner in partners:
        pl.semaphore_signal(barrier, inc=1, device_id=partner, device_id_type=MESH)

    def elementwise(i, _):
        rows = pl.ds(pl.multiple_of(i * 64, 64), 64)
        g = gate_ref[rows, :].astype(F32)
        u = up_ref[rows, :].astype(F32)
        h = dh_ref[rows, :].astype(F32)
        s = 1.0 / (1.0 + jnp.exp(-g))
        dga[tensor, 0, y_lo, rows, :] = (h * u * s * (1.0 + g * (1.0 - s))).astype(BF16)
        dga[tensor, 1, y_lo, rows, :] = (h * g * s).astype(BF16)
        return 0

    for load in loads[:3]:
        load.wait()
    lax.fori_loop(0, 8, elementwise, 0)
    pl.semaphore_wait(barrier, len(partners))

    def dg(y_from, m):
        return dga.at[lax.div(y_from, 2) * 2 + core, m, lax.rem(y_from, 2)]

    def along(y_from, m, index, y_to):
        send(dg(y_from, m), dg(y_from, m), dg_send, dg_recv.at[index], device(x, y_to, z, core))

    def cross(y_from, m):
        send(dg(y_from, m), dg(y_from, m), dx_send, dx_recv, device(x, y, z, other))

    along(y, 0, 0, yp)
    along(y, 1, 1, ym)
    along(y, 1, 2, yp)
    along(y, 0, 3, ym)
    cross(y, 0)
    cross(y, 1)

    loads[3].wait()
    l_core = lax.div(x, 2)
    l_slot = lax.rem(x, 2) * 2 + y_lo
    for x_t in range(NX):
        is_me = jnp.logical_and(jnp.logical_and(x == x_t, y == y_t), core == l_core)
        l1[x_t] = left_ref[:, x_t // 2, x_t % 2]
        send_or_copy(is_me, l1.at[x_t], lb.at[z, l_slot], l1_send, l1_recv,
                     device(x_t, y_t, z, l_core))

    loads[4].wait()

    def transpose(y_to, _):
        for bl in range(2):
            for cc in range(2):
                for part_of in range(4):
                    column = pl.multiple_of(
                        y_to * 2048 + (bl * 1024 + cc * 512 + part_of * 128), 128
                    )
                    tt[y_to, bl, cc, part_of * 128:(part_of + 1) * 128] = (
                        tok_ref[:, pl.ds(column, 128)].T
                    )
        return 0

    lax.fori_loop(0, NY, transpose, 0)

    def rows_of(kc):
        return pl.ds(STARTS[kc], SIZES[kc])

    def send_tokens(kc):
        rows = rows_of(kc)
        here = tk.at[:, rows, pl.ds(lane_of(y, core), 128)]
        send(tt.at[yo, 0, :, rows], fw.at[0, :, rows], tk_send, fw_recv.at[kc, 0],
             device(x, yp, z, core))
        send(tt.at[yo, 1, :, rows], fw.at[1, :, rows], tk_send, fw_recv.at[kc, 1],
             device(x, ym, z, core))
        for cc in range(2):
            send(tt.at[yp, :, cc, rows], here, tk_send, tk_recv.at[kc], device(x, yp, z, cc))
            send(tt.at[ym, :, cc, rows], here, tk_send, tk_recv.at[kc], device(x, ym, z, cc))
        send(tt.at[y, :, other, rows], here, tk_send, tk_recv.at[kc], device(x, y, z, other))
        pltpu.make_async_copy(tt.at[y, :, core, rows], here, tk_recv.at[kc]).start()

    def forward(kc):
        rows = rows_of(kc)
        for way, y_from, y_to in ((0, ym, yp), (1, yp, ym)):
            arrived(fw.at[way, :, rows], fw_recv.at[kc, way])
            there = tk.at[way, rows, pl.ds(lane_of(y_from, core), 128)]
            for cc in range(2):
                send(fw.at[way, cc, rows], there, tf_send, tk_recv.at[kc],
                     device(x, y_to, z, cc))

    arrived(dg(ym, 0), dg_recv.at[0])
    along(ym, 0, 4, yp)
    arrived(dg(yp, 1), dg_recv.at[1])
    along(yp, 1, 5, ym)
    cross(ym, 0)
    cross(yp, 1)

    zp, zm = ring(z, 1, NZ), ring(z, -1, NZ)

    def left_up(step):
        slot = ring(z, -step, NZ)
        if step > 0:
            arrived(lb.at[slot], l3_recv.at[step - 1])
        if step < 4:
            send(lb.at[slot], lb.at[slot], l3_send, l3_recv.at[step],
                 device(x, y, zp, core))

    def left_down(step):
        slot = ring(z, step, NZ)
        if step > 0:
            arrived(lb.at[slot], l3_recv.at[3 + step])
        if step < 3:
            send(lb.at[slot], lb.at[slot], l3_send, l3_recv.at[4 + step],
                 device(x, y, zm, core))

    arrived(lb.at[z], l1_recv)

    def left_step(step):
        left_up(step)
        if step < 4:
            left_down(step)

    send_tokens(0)
    left_step(0)
    arrived(dg(ym, 1), dg_recv.at[2])
    cross(ym, 1)
    arrived(dg(yp, 0), dg_recv.at[3])
    cross(yp, 0)
    left_step(1)

    arrived(dg(yo, 0), dg_recv.at[4])
    cross(yo, 0)
    arrived(dg(yo, 1), dg_recv.at[5])
    cross(yo, 1)
    forward(0)
    send_tokens(1)
    left_step(2)
    arrived(dga.at[0:2], dx_recv)

    def multiply(kc):
        rows, size = rows_of(kc), SIZES[kc]
        arrived(tk.at[:, rows], tk_recv.at[kc])

        def matrix(m, _):
            for t in range(4):
                total = jnp.dot(
                    tk[:, rows].reshape(2 * size, 1024), dga[t, m].reshape(1024, 256),
                    preferred_element_type=F32,
                )
                for bl in range(2):
                    part[bl * 2 + m, rows, t * 256:(t + 1) * 256] = (
                        total[bl * size:(bl + 1) * size]
                    )
            return 0

        lax.fori_loop(0, 2, matrix, 0)

    def halves(kc):
        start, half = STARTS[kc], SIZES[kc] // 2
        return pl.ds(start, half), pl.ds(start + half, half), pl.ds(start // 2, half)

    def reduce_far(kc):
        rows = rows_of(kc)
        first, second, packed = halves(kc)
        a_s[rows] = part[xo, rows].astype(BF16)
        send(a_s.at[first], a_r.at[0, packed], a_send, a_recv.at[kc, 0],
             device(xp, y, z, core))
        send(a_s.at[second], a_r.at[1, packed], a_send, a_recv.at[kc, 1],
             device(xm1, y, z, core))

    def reduce_near(kc):
        rows = rows_of(kc)
        first, second, packed = halves(kc)
        arrived(a_r.at[0, packed], a_recv.at[kc, 0])
        b_s[0, first] = (part[xp, first] + a_r[0, packed].astype(F32)).astype(BF16)
        b_s[0, second] = part[xp, second].astype(BF16)
        send(b_s.at[0, rows], b_r.at[0, rows], bb_send, bb_recv.at[kc],
             device(xp, y, z, core))
        arrived(a_r.at[1, packed], a_recv.at[kc, 1])
        b_s[1, first] = part[xm1, first].astype(BF16)
        b_s[1, second] = (part[xm1, second] + a_r[1, packed].astype(F32)).astype(BF16)
        send(b_s.at[1, rows], b_r.at[1, rows], bb_send, bb_recv.at[kc],
             device(xm1, y, z, core))

    def reduce_own(kc):
        rows = rows_of(kc)
        arrived(b_r.at[:, rows], bb_recv.at[kc])
        for zt in range(NZ):
            cols = slice(zt * 128, (zt + 1) * 128)
            z_s[zt, rows] = (
                part[x, rows, cols]
                + b_r[0, rows, cols].astype(F32)
                + b_r[1, rows, cols].astype(F32)
            ).astype(BF16)
        for step in range(1, NZ):
            zt = ring(z, step, NZ)
            send(z_s.at[zt, rows], z_r.at[step - 1, rows], zz_send,
                 zz_recv.at[kc], device(x, y, zt, core))

    def reduce_z(kc):
        rows = rows_of(kc)
        arrived(z_r.at[:, rows], zz_recv.at[kc])
        total = z_s[z, rows].astype(F32)
        for i in range(NZ - 1):
            total = total + z_r[i, rows].astype(F32)
        g_full[core, rows] = total.astype(BF16)
        send(g_full.at[core, rows], g_full.at[core, rows], g_send, g_recv.at[kc],
             device(x, y, z, other))

    far = (1 - y_hi) * 2

    def right_send(_):
        loads[5].wait()
        send(rm.at[tensor], rm.at[tensor], r_send, r_recv.at[0],
             device(x, NY - 1 - y, z, core))
        send(rm.at[tensor], rm.at[tensor], r_send, r_recv.at[1],
             device(x, y, z, other))

    def right_cross(_):
        arrived(rm.at[far + core], r_recv.at[0])
        send(rm.at[far + core], rm.at[far + core], r_send, r_recv.at[2],
             device(x, y, z, other))

    def left_times(low, high):
        return sum(
            jnp.dot(
                lb[:, :, :, cc * HALF + low:cc * HALF + high].reshape(512, high - low),
                g_full[cc, low:high], preferred_element_type=F32,
            )
            for cc in range(2)
        )

    def left_most(_):
        for kc in range(3):
            arrived(g_full.at[other, rows_of(kc)], g_recv.at[kc])
        lg_f[...] = left_times(0, 384)

    M, A, B, C, Z = multiply, reduce_far, reduce_near, reduce_own, reduce_z
    F, T = forward, send_tokens
    order = (
        (M, 0), (A, 0), (left_step, 3), (F, 1), (T, 2), (B, 0),
        (M, 1), (A, 1), (left_step, 4), (F, 2), (T, 3), (B, 1), (C, 0),
        (M, 2), (A, 2), (F, 3), (right_send, 0), (B, 2), (C, 1), (Z, 0),
        (M, 3), (A, 3), (C, 2), (Z, 1), (B, 3), (right_cross, 0),
        (C, 3), (Z, 2), (left_most, 0), (Z, 3),
    )
    for step, kc in order:
        step(kc)

    for kc in range(3, CHUNKS):
        arrived(g_full.at[other, rows_of(kc)], g_recv.at[kc])
    product = lg_f[...] + left_times(384, HALF)
    lg_s[...] = product.astype(BF16).reshape(NZ, 64, 128)

    place = pl.ds(pl.multiple_of(z * 128, 128), 128)
    for step in range(1, NZ):
        zt = ring(z, step, NZ)
        send(lg_s.at[zt], xm.at[:, place], t1_send, t1_recv,
             device(x, y, zt, core))
    xm[:, place] = lg_s[z]
    arrived(rm.at[y_hi * 2 + other], r_recv.at[1])
    arrived(rm.at[far + other], r_recv.at[2])
    arrived(lg_s.at[0:NZ - 1], t1_recv)

    block = 2 * y + lax.div(x, 2)
    for yh in range(2):
        for cc in range(2):
            t = yh * 2 + cc
            result = jnp.dot(
                xm[...], rm[:, :, t * 256:(t + 1) * 256].reshape(1024, 256),
                preferred_element_type=F32,
            )
            out_s[t * 4:t * 4 + 4] = result.reshape(4, 16, 256)
            for xl in range(2):
                for yl in range(2):
                    is_me = jnp.logical_and(
                        jnp.logical_and(x == 2 * core + xl, y == 2 * yh + yl), core == cc
                    )
                    piece = xl * 2 + yl
                    send_or_copy(is_me, out_s.at[t * 4 + piece], out_ref.at[mine, block],
                                 t2_send, t2_recv, device(2 * core + xl, 2 * yh + yl, z, cc))

    sent(tt.at[0:3], tk_send)
    sent(tt.at[3, 0], tk_send)
    sent(fw, tf_send)
    sent(dga.at[0], dg_send)
    sent(dga.at[0, 0], dg_send)
    sent(dga.at[0:2], dx_send)
    sent(a_s, a_send)
    sent(b_s, bb_send)
    sent(z_s.at[0:NZ - 1], zz_send)
    sent(g_full.at[0], g_send)
    sent(lb.at[0:NZ - 1], l3_send)
    sent(rm.at[0:3], r_send)
    sent(lg_s.at[0:NZ - 1], t1_send)
    sent(l1.at[0:3], l1_send)
    pl.when(jnp.logical_not(jnp.logical_and(y == y_t, core == l_core)))(
        lambda: sent(l1.at[3], l1_send)
    )
    arrived(out_ref, t2_recv)
    sent(out_s.at[0:15], t2_send)
    pl.when(core != l_core)(lambda: sent(out_s.at[15], t2_send))


def local(tokens, gate_pre, up_pre, d_hidden, left_roots, right_roots):
    dma = pltpu.SemaphoreType.DMA
    vm = pltpu.VMEM
    scratch = [
        vm((128, 8192), BF16), vm((512, 256), BF16), vm((512, 256), BF16),
        vm((512, 256), BF16), vm((16, 2, 2, 1024), BF16),
        vm((4, 2, 2, 512, 256), BF16),
        vm((NY, 2, 2, HALF, 128), BF16),
        vm((2, HALF, 1024), BF16),
        vm((2, 2, HALF, 128), BF16),
        vm((4, HALF, 1024), F32),
        vm((HALF, 1024), BF16),
        vm((2, HALF // 2, 1024), BF16),
        vm((2, HALF, 1024), BF16),
        vm((2, HALF, 1024), BF16),
        vm((NZ, HALF, 128), BF16),
        vm((NZ - 1, HALF, 128), BF16),
        vm((2, HALF, 128), BF16),
        vm((4, 16, 1024), BF16),
        vm((NZ, 4, 16, 1024), BF16),
        vm((512, 128), F32),
        vm((NZ, 64, 128), BF16),
        vm((64, 1024), BF16),
        vm((4, 256, 1024), BF16),
        vm((16, 16, 256), F32),
        dma, dma((6,)), dma, dma,
        dma, dma((CHUNKS,)), dma,
        dma((CHUNKS, 2)),
        dma, dma((CHUNKS, 2)), dma, dma((CHUNKS,)),
        dma, dma((CHUNKS,)), dma, dma((CHUNKS,)),
        dma, dma, dma, dma((NZ - 1,)), dma, dma((3,)),
        dma, dma, dma, dma, dma((6,)),
    ]
    out = pl.pallas_call(
        kernel,
        out_shape=jax.ShapeDtypeStruct((2, 8, 16, 256), F32),
        in_specs=[pl.BlockSpec(memory_space=pltpu.HBM)] * 6,
        out_specs=pl.BlockSpec(memory_space=pltpu.VMEM),
        scratch_shapes=scratch,
        compiler_params=pltpu.CompilerParams(
            collective_id=0, has_side_effects=True, vmem_limit_bytes=60 * 1024 * 1024
        ),
        cost_estimate=pl.CostEstimate(
            flops=4_500_000_000, bytes_accessed=8_000_000, transcendentals=131072
        ),
    )(tokens, gate_pre, up_pre, d_hidden, left_roots, right_roots)
    return out.transpose(2, 1, 0, 3)


def solution(mesh):
    in_specs = (
        P(("dp", "tensor"), None),
        P("dp", "tensor"),
        P("dp", "tensor"),
        P("dp", "tensor"),
        P("dp", None, None, None),
        P(None, "tensor", None),
    )
    out_specs = P("dp", None, None, "tensor")
    return jax.shard_map(local, mesh=mesh, in_specs=in_specs, out_specs=out_specs, check_vma=False)
```

time: 845 us -> 102 us (0.12)
  the two profiles are of different devices: /device:TPU:16 before, /device:TPU:1 now
where the time goes in v1:
time: 102 us
  Pallas kernels  100 us (98%)
  local copies, waits for them, and re-layouts  1.86 us (2%)
    pallas_call x1, Pallas kernels, local(): pl.pallas_call(kernel, out_shape=jax.ShapeDtypeStruct((2, 8, 16, 256), F3...  100 us

profile of v1, /device:TPU:1, one launch (start us, length us, event | category | flops | bytes accessed | tf_op | source)
XLA Modules:
  0.0 102.1 jit_solution(8767165299220842399)
XLA Ops:
  0.0 100.3 %shard_map.64 = f32[2,8,16,256]{3,2,1,0:T(8,128)} custom-call(bf16[128,8192]{1,0:T(8,128)(2,1)} %tok_hbm.1, bf16[512,256]{1,0:T(8,128)(2,1)} %gate_hbm.1, bf16[512,256]{1,0:T(8,128)(2,1)} %up_hbm.1, bf16[512,256]{1,0:T(8,128)(2,1)} %dh_hbm.1, bf16[16,8,2,1024]{3,2,1,0:T(2,128)(2,1)} %left_hbm.1, bf16[2,256,1024]{2,1,0:T(8,128)(2,1)} %right_hbm.1), custom_call_target="tpu_custom_call" | custom-call | flops 4499999744 | bytes 8000000 | tf_op jit(solution)/shard_map/pallas_call | solution.py:436
  100.3 1.9 %copy.7 = f32[16,8,2,256]{3,2,1,0:T(2,128)} copy(f32[16,8,2,256]{3,0,1,2:T(8,128)} %bitcast.1) | data formatting | bytes 524288 | tf_op jit(solution)/shard_map/transpose | solution.py:449

commit v2 on v1

--- a/solution.py
+++ b/solution.py
@@ -10,7 +10,7 @@
 BF16 = jnp.bfloat16
 
 NX, NY, NZ = 4, 4, 8
-SIZES = (96, 160, 160, 96)
+SIZES = (96, 128, 128, 96, 64)
 STARTS = tuple(sum(SIZES[:i]) for i in range(len(SIZES)))
 CHUNKS = len(SIZES)
 HALF = 512
@@ -211,14 +211,13 @@
             send(lb.at[slot], lb.at[slot], l3_send, l3_recv.at[4 + step],
                  device(x, y, zm, core))
 
-    arrived(lb.at[z], l1_recv)
-
     def left_step(step):
         left_up(step)
         if step < 4:
             left_down(step)
 
     send_tokens(0)
+    arrived(lb.at[z], l1_recv)
     left_step(0)
     arrived(dg(ym, 1), dg_recv.at[2])
     cross(ym, 1)
@@ -233,13 +232,13 @@
     forward(0)
     send_tokens(1)
     left_step(2)
-    arrived(dga.at[0:2], dx_recv)
 
     def multiply(kc):
         rows, size = rows_of(kc), SIZES[kc]
         arrived(tk.at[:, rows], tk_recv.at[kc])
 
-        def matrix(m, _):
+        def matrix(turn, _):
+            m = lax.rem(mine + turn, 2)
             for t in range(4):
                 total = jnp.dot(
                     tk[:, rows].reshape(2 * size, 1024), dga[t, m].reshape(1024, 256),
@@ -249,6 +248,7 @@
                     part[bl * 2 + m, rows, t * 256:(t + 1) * 256] = (
                         total[bl * size:(bl + 1) * size]
                     )
+            pl.when(turn == 0)(lambda: reduce_far(kc))
             return 0
 
         lax.fori_loop(0, 2, matrix, 0)
@@ -266,19 +266,22 @@
         send(a_s.at[second], a_r.at[1, packed], a_send, a_recv.at[kc, 1],
              device(xm1, y, z, core))
 
-    def reduce_near(kc):
-        rows = rows_of(kc)
+    def near_plain(kc):
+        first, second, _ = halves(kc)
+        for way, x_to, plain in ((0, xp, second), (1, xm1, first)):
+            b_s[way, plain] = part[x_to, plain].astype(BF16)
+            send(b_s.at[way, plain], b_r.at[way, plain], bb_send, bb_recv.at[kc],
+                 device(x_to, y, z, core))
+
+    def near_sum(kc):
         first, second, packed = halves(kc)
-        arrived(a_r.at[0, packed], a_recv.at[kc, 0])
-        b_s[0, first] = (part[xp, first] + a_r[0, packed].astype(F32)).astype(BF16)
-        b_s[0, second] = part[xp, second].astype(BF16)
-        send(b_s.at[0, rows], b_r.at[0, rows], bb_send, bb_recv.at[kc],
-             device(xp, y, z, core))
-        arrived(a_r.at[1, packed], a_recv.at[kc, 1])
-        b_s[1, first] = part[xm1, first].astype(BF16)
-        b_s[1, second] = (part[xm1, second] + a_r[1, packed].astype(F32)).astype(BF16)
-        send(b_s.at[1, rows], b_r.at[1, rows], bb_send, bb_recv.at[kc],
-             device(xm1, y, z, core))
+        for way, x_to, summed in ((0, xp, first), (1, xm1, second)):
+            arrived(a_r.at[way, packed], a_recv.at[kc, way])
+            b_s[way, summed] = (
+                part[x_to, summed] + a_r[way, packed].astype(F32)
+            ).astype(BF16)
+            send(b_s.at[way, summed], b_r.at[way, summed], bb_send, bb_recv.at[kc],
+                 device(x_to, y, z, core))
 
     def reduce_own(kc):
         rows = rows_of(kc)
@@ -329,23 +332,27 @@
         )
 
     def left_most(_):
-        for kc in range(3):
+        for kc in range(4):
             arrived(g_full.at[other, rows_of(kc)], g_recv.at[kc])
         lg_f[...] = left_times(0, 384)
 
-    M, A, B, C, Z = multiply, reduce_far, reduce_near, reduce_own, reduce_z
+    def gathered(_):
+        arrived(dga.at[0:2], dx_recv)
+
+    M, B, S, C, Z = multiply, near_plain, near_sum, reduce_own, reduce_z
     F, T = forward, send_tokens
     order = (
-        (M, 0), (A, 0), (left_step, 3), (F, 1), (T, 2), (B, 0),
-        (M, 1), (A, 1), (left_step, 4), (F, 2), (T, 3), (B, 1), (C, 0),
-        (M, 2), (A, 2), (F, 3), (right_send, 0), (B, 2), (C, 1), (Z, 0),
-        (M, 3), (A, 3), (C, 2), (Z, 1), (B, 3), (right_cross, 0),
-        (C, 3), (Z, 2), (left_most, 0), (Z, 3),
+        (F, 1), (T, 2), (gathered, 0), (M, 0), (B, 0), (left_step, 3), (S, 0),
+        (F, 2), (T, 3), (M, 1), (B, 1), (left_step, 4), (S, 1), (C, 0),
+        (F, 3), (T, 4), (M, 2), (B, 2), (S, 2), (C, 1), (Z, 0),
+        (F, 4), (right_send, 0), (M, 3), (B, 3), (S, 3), (C, 2), (Z, 1),
+        (M, 4), (B, 4), (S, 4), (C, 3), (Z, 2), (right_cross, 0),
+        (C, 4), (Z, 3), (left_most, 0), (Z, 4),
     )
     for step, kc in order:
         step(kc)
 
-    for kc in range(3, CHUNKS):
+    for kc in range(4, CHUNKS):
         arrived(g_full.at[other, rows_of(kc)], g_recv.at[kc])
     product = lg_f[...] + left_times(384, HALF)
     lg_s[...] = product.astype(BF16).reshape(NZ, 64, 128)

time: 102 us -> 97.9 us (0.960)
  Pallas kernels: 100 us -> 95.9 us
    pallas_call x1, Pallas kernels: 100 us -> 95.9 us  [local(): pl.pallas_call(kernel, out_shape=jax.ShapeDtypeStruct((2, 8, 16, 256), F3...]
where the time goes in v2:
time: 97.9 us; the launch traced here: 97.8 us
  Pallas kernels  95.9 us (98%)
  local copies, waits for them, and re-layouts  1.86 us (2%)
    pallas_call x1, Pallas kernels, local(): pl.pallas_call(kernel, out_shape=jax.ShapeDtypeStruct((2, 8, 16, 256), F3...  95.9 us

profile of v2, /device:TPU:1, one launch (start us, length us, event | category | flops | bytes accessed | tf_op | source)
XLA Modules:
  0.0 97.8 jit_solution(5016807506714286393)
XLA Ops:
  0.0 95.9 %shard_map.64 = f32[2,8,16,256]{3,2,1,0:T(8,128)} custom-call(bf16[128,8192]{1,0:T(8,128)(2,1)} %tok_hbm.1, bf16[512,256]{1,0:T(8,128)(2,1)} %gate_hbm.1, bf16[512,256]{1,0:T(8,128)(2,1)} %up_hbm.1, bf16[512,256]{1,0:T(8,128)(2,1)} %dh_hbm.1, bf16[16,8,2,1024]{3,2,1,0:T(2,128)(2,1)} %left_hbm.1, bf16[2,256,1024]{2,1,0:T(8,128)(2,1)} %right_hbm.1), custom_call_target="tpu_custom_call" | custom-call | flops 4499999744 | bytes 8000000 | tf_op jit(solution)/shard_map/pallas_call | solution.py:443
  95.9 1.9 %copy.7 = f32[16,8,2,256]{3,2,1,0:T(2,128)} copy(f32[16,8,2,256]{3,0,1,2:T(8,128)} %bitcast.1) | data formatting | bytes 524288 | tf_op jit(solution)/shard_map/transpose | solution.py:456

commit v3 on v2

--- a/solution.py
+++ b/solution.py
@@ -10,10 +10,11 @@
 BF16 = jnp.bfloat16
 
 NX, NY, NZ = 4, 4, 8
-SIZES = (96, 128, 128, 96, 64)
+SIZES = (96, 128, 128, 128, 32)
 STARTS = tuple(sum(SIZES[:i]) for i in range(len(SIZES)))
 CHUNKS = len(SIZES)
 HALF = 512
+FAR_FIRST = (4, 3, 5, 2, 6, 1, 7)
 
 
 def device(x, y, z, core):
@@ -293,7 +294,7 @@
                 + b_r[0, rows, cols].astype(F32)
                 + b_r[1, rows, cols].astype(F32)
             ).astype(BF16)
-        for step in range(1, NZ):
+        for step in FAR_FIRST:
             zt = ring(z, step, NZ)
             send(z_s.at[zt, rows], z_r.at[step - 1, rows], zz_send,
                  zz_recv.at[kc], device(x, y, zt, core))
@@ -322,10 +323,12 @@
         send(rm.at[far + core], rm.at[far + core], r_send, r_recv.at[2],
              device(x, y, z, other))
 
-    def left_times(low, high):
+    def left_times(way, low, high):
         return sum(
             jnp.dot(
-                lb[:, :, :, cc * HALF + low:cc * HALF + high].reshape(512, high - low),
+                lb[:, 2 * way:2 * way + 2, :, cc * HALF + low:cc * HALF + high].reshape(
+                    256, high - low
+                ),
                 g_full[cc, low:high], preferred_element_type=F32,
             )
             for cc in range(2)
@@ -334,7 +337,8 @@
     def left_most(_):
         for kc in range(4):
             arrived(g_full.at[other, rows_of(kc)], g_recv.at[kc])
-        lg_f[...] = left_times(0, 384)
+        for way in range(2):
+            lg_f[way] = left_times(way, 0, 384)
 
     def gathered(_):
         arrived(dga.at[0:2], dx_recv)
@@ -354,35 +358,37 @@
 
     for kc in range(4, CHUNKS):
         arrived(g_full.at[other, rows_of(kc)], g_recv.at[kc])
-    product = lg_f[...] + left_times(384, HALF)
-    lg_s[...] = product.astype(BF16).reshape(NZ, 64, 128)
-
     place = pl.ds(pl.multiple_of(z * 128, 128), 128)
-    for step in range(1, NZ):
-        zt = ring(z, step, NZ)
-        send(lg_s.at[zt], xm.at[:, place], t1_send, t1_recv,
-             device(x, y, zt, core))
-    xm[:, place] = lg_s[z]
+    for way in range(2):
+        some = slice(32 * way, 32 * way + 32)
+        product = lg_f[way] + left_times(way, 384, HALF)
+        lg_s[:, some] = product.astype(BF16).reshape(NZ, 32, 128)
+        for step in FAR_FIRST:
+            zt = ring(z, step, NZ)
+            send(lg_s.at[zt, some], xm.at[some, place], t1_send, t1_recv.at[way],
+                 device(x, y, zt, core))
+        xm[some, place] = lg_s[z, some]
     arrived(rm.at[y_hi * 2 + other], r_recv.at[1])
     arrived(rm.at[far + other], r_recv.at[2])
-    arrived(lg_s.at[0:NZ - 1], t1_recv)
 
     block = 2 * y + lax.div(x, 2)
-    for yh in range(2):
-        for cc in range(2):
-            t = yh * 2 + cc
-            result = jnp.dot(
-                xm[...], rm[:, :, t * 256:(t + 1) * 256].reshape(1024, 256),
-                preferred_element_type=F32,
-            )
-            out_s[t * 4:t * 4 + 4] = result.reshape(4, 16, 256)
-            for xl in range(2):
+    for xl in range(2):
+        some = slice(32 * xl, 32 * xl + 32)
+        arrived(lg_s.at[0:NZ - 1, some], t1_recv.at[xl])
+        for yh in range(2):
+            for cc in range(2):
+                t = yh * 2 + cc
+                result = jnp.dot(
+                    xm[some], rm[:, :, t * 256:(t + 1) * 256].reshape(1024, 256),
+                    preferred_element_type=F32,
+                )
+                first = xl * 8 + t * 2
+                out_s[first:first + 2] = result.reshape(2, 16, 256)
                 for yl in range(2):
                     is_me = jnp.logical_and(
                         jnp.logical_and(x == 2 * core + xl, y == 2 * yh + yl), core == cc
                     )
-                    piece = xl * 2 + yl
-                    send_or_copy(is_me, out_s.at[t * 4 + piece], out_ref.at[mine, block],
+                    send_or_copy(is_me, out_s.at[first + yl], out_ref.at[mine, block],
                                  t2_send, t2_recv, device(2 * core + xl, 2 * yh + yl, z, cc))
 
     sent(tt.at[0:3], tk_send)
@@ -427,7 +433,7 @@
         vm((2, HALF, 128), BF16),
         vm((4, 16, 1024), BF16),
         vm((NZ, 4, 16, 1024), BF16),
-        vm((512, 128), F32),
+        vm((2, 256, 128), F32),
         vm((NZ, 64, 128), BF16),
         vm((64, 1024), BF16),
         vm((4, 256, 1024), BF16),
@@ -438,7 +444,7 @@
         dma, dma((CHUNKS, 2)), dma, dma((CHUNKS,)),
         dma, dma((CHUNKS,)), dma, dma((CHUNKS,)),
         dma, dma, dma, dma((NZ - 1,)), dma, dma((3,)),
-        dma, dma, dma, dma, dma((6,)),
+        dma, dma((2,)), dma, dma, dma((6,)),
     ]
     out = pl.pallas_call(
         kernel,

time: 97.9 us -> 96.5 us (0.986)
  Pallas kernels: 95.9 us -> 94.6 us
    pallas_call x1, Pallas kernels: 95.9 us -> 94.6 us  [local(): pl.pallas_call(kernel, out_shape=jax.ShapeDtypeStruct((2, 8, 16, 256), F3...]
where the time goes in v3:
time: 96.5 us; the launch traced here: 96.4 us
  Pallas kernels  94.6 us (98%)
  local copies, waits for them, and re-layouts  1.86 us (2%)
    pallas_call x1, Pallas kernels, local(): pl.pallas_call(kernel, out_shape=jax.ShapeDtypeStruct((2, 8, 16, 256), F3...  94.6 us

profile of v3, /device:TPU:1, one launch (start us, length us, event | category | flops | bytes accessed | tf_op | source)
XLA Modules:
  0.0 96.4 jit_solution(12103119116129436618)
XLA Ops:
  0.0 94.6 %shard_map.64 = f32[2,8,16,256]{3,2,1,0:T(8,128)} custom-call(bf16[128,8192]{1,0:T(8,128)(2,1)} %tok_hbm.1, bf16[512,256]{1,0:T(8,128)(2,1)} %gate_hbm.1, bf16[512,256]{1,0:T(8,128)(2,1)} %up_hbm.1, bf16[512,256]{1,0:T(8,128)(2,1)} %dh_hbm.1, bf16[16,8,2,1024]{3,2,1,0:T(2,128)(2,1)} %left_hbm.1, bf16[2,256,1024]{2,1,0:T(8,128)(2,1)} %right_hbm.1), custom_call_target="tpu_custom_call" | custom-call | flops 4499999744 | bytes 8000000 | tf_op jit(solution)/shard_map/pallas_call | solution.py:449
  94.6 1.9 %copy.7 = f32[16,8,2,256]{3,2,1,0:T(2,128)} copy(f32[16,8,2,256]{3,0,1,2:T(8,128)} %bitcast.1) | data formatting | bytes 524288 | tf_op jit(solution)/shard_map/transpose | solution.py:462

commit v4 on v3

--- a/solution.py
+++ b/solution.py
@@ -249,7 +249,14 @@
                     part[bl * 2 + m, rows, t * 256:(t + 1) * 256] = (
                         total[bl * size:(bl + 1) * size]
                     )
-            pl.when(turn == 0)(lambda: reduce_far(kc))
+
+            @pl.when(turn == 0)
+            def _():
+                reduce_far(kc)
+                if kc < 2:
+                    forward(kc + 1)
+                    send_tokens(kc + 2)
+
             return 0
 
         lax.fori_loop(0, 2, matrix, 0)
@@ -346,8 +353,8 @@
     M, B, S, C, Z = multiply, near_plain, near_sum, reduce_own, reduce_z
     F, T = forward, send_tokens
     order = (
-        (F, 1), (T, 2), (gathered, 0), (M, 0), (B, 0), (left_step, 3), (S, 0),
-        (F, 2), (T, 3), (M, 1), (B, 1), (left_step, 4), (S, 1), (C, 0),
+        (gathered, 0), (M, 0), (B, 0), (left_step, 3), (S, 0),
+        (M, 1), (B, 1), (left_step, 4), (S, 1), (C, 0),
         (F, 3), (T, 4), (M, 2), (B, 2), (S, 2), (C, 1), (Z, 0),
         (F, 4), (right_send, 0), (M, 3), (B, 3), (S, 3), (C, 2), (Z, 1),
         (M, 4), (B, 4), (S, 4), (C, 3), (Z, 2), (right_cross, 0),

time: 96.5 us -> 96.5 us (level)
  no operation moved by 1% of the time
where the time goes in v4:
time: 96.5 us; the launch traced here: 96.4 us
  Pallas kernels  94.5 us (98%)
  local copies, waits for them, and re-layouts  1.86 us (2%)
    pallas_call x1, Pallas kernels, local(): pl.pallas_call(kernel, out_shape=jax.ShapeDtypeStruct((2, 8, 16, 256), F3...  94.5 us

profile of v4, /device:TPU:1, one launch (start us, length us, event | category | flops | bytes accessed | tf_op | source)
XLA Modules:
  0.0 96.4 jit_solution(11996391008430697508)
XLA Ops:
  0.0 94.5 %shard_map.64 = f32[2,8,16,256]{3,2,1,0:T(8,128)} custom-call(bf16[128,8192]{1,0:T(8,128)(2,1)} %tok_hbm.1, bf16[512,256]{1,0:T(8,128)(2,1)} %gate_hbm.1, bf16[512,256]{1,0:T(8,128)(2,1)} %up_hbm.1, bf16[512,256]{1,0:T(8,128)(2,1)} %dh_hbm.1, bf16[16,8,2,1024]{3,2,1,0:T(2,128)(2,1)} %left_hbm.1, bf16[2,256,1024]{2,1,0:T(8,128)(2,1)} %right_hbm.1), custom_call_target="tpu_custom_call" | custom-call | flops 4499999744 | bytes 8000000 | tf_op jit(solution)/shard_map/pallas_call | solution.py:456
  94.5 1.9 %copy.7 = f32[16,8,2,256]{3,2,1,0:T(2,128)} copy(f32[16,8,2,256]{3,0,1,2:T(8,128)} %bitcast.1) | data formatting | bytes 524288 | tf_op jit(solution)/shard_map/transpose | solution.py:469

commit v5 on v4

--- a/solution.py
+++ b/solution.py
@@ -390,7 +390,7 @@
                     preferred_element_type=F32,
                 )
                 first = xl * 8 + t * 2
-                out_s[first:first + 2] = result.reshape(2, 16, 256)
+                out_s[first:first + 2] = result.astype(BF16).reshape(2, 16, 256)
                 for yl in range(2):
                     is_me = jnp.logical_and(
                         jnp.logical_and(x == 2 * core + xl, y == 2 * yh + yl), core == cc
@@ -444,7 +444,7 @@
         vm((NZ, 64, 128), BF16),
         vm((64, 1024), BF16),
         vm((4, 256, 1024), BF16),
-        vm((16, 16, 256), F32),
+        vm((16, 16, 256), BF16),
         dma, dma((6,)), dma, dma,
         dma, dma((CHUNKS,)), dma,
         dma((CHUNKS, 2)),
@@ -455,7 +455,7 @@
     ]
     out = pl.pallas_call(
         kernel,
-        out_shape=jax.ShapeDtypeStruct((2, 8, 16, 256), F32),
+        out_shape=jax.ShapeDtypeStruct((2, 8, 16, 256), BF16),
         in_specs=[pl.BlockSpec(memory_space=pltpu.HBM)] * 6,
         out_specs=pl.BlockSpec(memory_space=pltpu.VMEM),
         scratch_shapes=scratch,
@@ -466,7 +466,7 @@
             flops=4_500_000_000, bytes_accessed=8_000_000, transcendentals=131072
         ),
     )(tokens, gate_pre, up_pre, d_hidden, left_roots, right_roots)
-    return out.transpose(2, 1, 0, 3)
+    return out.transpose(2, 1, 0, 3).astype(F32)
 
 
 def solution(mesh):

time: 96.5 us -> 95.9 us (level)
    transpose x1 -> x0, local copies, waits for them, and re-layouts: 1.86 us -> none  [local(): return out.transpose(2, 1, 0, 3)]
where the time goes in v5:
time: 95.9 us; the launch traced here: 95.8 us
  Pallas kernels  93.9 us (98%)
    pallas_call x1, Pallas kernels, local(): pl.pallas_call(kernel, out_shape=jax.ShapeDtypeStruct((2, 8, 16, 256), BF...  93.9 us

profile of v5, /device:TPU:1, one launch (start us, length us, event | category | flops | bytes accessed | tf_op | source)
XLA Modules:
  0.0 95.8 jit_solution(11191967896794853105)
XLA Ops:
  0.0 93.9 %shard_map.64 = bf16[2,8,16,256]{3,2,1,0:T(8,128)(2,1)} custom-call(bf16[128,8192]{1,0:T(8,128)(2,1)} %tok_hbm.1, bf16[512,256]{1,0:T(8,128)(2,1)} %gate_hbm.1, bf16[512,256]{1,0:T(8,128)(2,1)} %up_hbm.1, bf16[512,256]{1,0:T(8,128)(2,1)} %dh_hbm.1, bf16[16,8,2,1024]{3,2,1,0:T(2,128)(2,1)} %left_hbm.1, bf16[2,256,1024]{2,1,0:T(8,128)(2,1)} %right_hbm.1), custom_call_target="tpu_custom_call" | custom-call | flops 4499999744 | bytes 8000000 | tf_op jit(solution)/shard_map/pallas_call | solution.py:456
  93.9 0.9 convert_bitcast_fusion
  94.9 0.9 copy.7

commit v6 on v4

--- a/solution.py
+++ b/solution.py
@@ -10,7 +10,7 @@
 BF16 = jnp.bfloat16
 
 NX, NY, NZ = 4, 4, 8
-SIZES = (96, 128, 128, 128, 32)
+SIZES = (96, 128, 128, 96, 64)
 STARTS = tuple(sum(SIZES[:i]) for i in range(len(SIZES)))
 CHUNKS = len(SIZES)
 HALF = 512

time: 96.5 us -> 94.9 us (0.983)
  Pallas kernels: 94.5 us -> 92.9 us
    pallas_call x1, Pallas kernels: 94.5 us -> 92.9 us  [local(): pl.pallas_call(kernel, out_shape=jax.ShapeDtypeStruct((2, 8, 16, 256), F3...]
where the time goes in v6:
time: 94.9 us; the launch traced here: 94.7 us
  Pallas kernels  92.9 us (98%)
  local copies, waits for them, and re-layouts  1.86 us (2%)
    pallas_call x1, Pallas kernels, local(): pl.pallas_call(kernel, out_shape=jax.ShapeDtypeStruct((2, 8, 16, 256), F3...  92.9 us

profile of v6, /device:TPU:1, one launch (start us, length us, event | category | flops | bytes accessed | tf_op | source)
XLA Modules:
  0.0 94.7 jit_solution(8742739907009066576)
XLA Ops:
  0.0 92.9 %shard_map.64 = f32[2,8,16,256]{3,2,1,0:T(8,128)} custom-call(bf16[128,8192]{1,0:T(8,128)(2,1)} %tok_hbm.1, bf16[512,256]{1,0:T(8,128)(2,1)} %gate_hbm.1, bf16[512,256]{1,0:T(8,128)(2,1)} %up_hbm.1, bf16[512,256]{1,0:T(8,128)(2,1)} %dh_hbm.1, bf16[16,8,2,1024]{3,2,1,0:T(2,128)(2,1)} %left_hbm.1, bf16[2,256,1024]{2,1,0:T(8,128)(2,1)} %right_hbm.1), custom_call_target="tpu_custom_call" | custom-call | flops 4499999744 | bytes 8000000 | tf_op jit(solution)/shard_map/pallas_call | solution.py:456
  92.9 1.9 %copy.7 = f32[16,8,2,256]{3,2,1,0:T(2,128)} copy(f32[16,8,2,256]{3,0,1,2:T(8,128)} %bitcast.1) | data formatting | bytes 524288 | tf_op jit(solution)/shard_map/transpose | solution.py:469

commit v7 on v6

--- a/solution.py
+++ b/solution.py
@@ -33,10 +33,10 @@
 
 def kernel(
     tok_hbm, gate_hbm, up_hbm, dh_hbm, left_hbm, right_hbm, out_ref,
-    tok_ref, gate_ref, up_ref, dh_ref, left_ref, dga, tt, tk, fw, part, a_s, a_r, b_s, b_r, z_s, z_r, g_full,
+    tok_ref, gate_ref, up_ref, dh_ref, left_ref, dga, tt, tk, fw, part, a_s, a_r, b_s, b_r, z_s, z_r, z_q, g_full,
     l1, lb, lg_f, lg_s, xm, rm, out_s,
     dg_send, dg_recv, dx_send, dx_recv, tk_send, tk_recv, tf_send,
-    fw_recv, a_send, a_recv, bb_send, bb_recv, zz_send, zz_recv,
+    fw_recv, a_send, a_recv, bb_send, bb_recv, zz_send, zz_recv, zq_recv,
     g_send, g_recv, l1_send, l1_recv, l3_send, l3_recv, r_send, r_recv,
     t1_send, t1_recv, t2_send, t2_recv, in_sem,
 ):
@@ -301,16 +301,30 @@
                 + b_r[0, rows, cols].astype(F32)
                 + b_r[1, rows, cols].astype(F32)
             ).astype(BF16)
-        for step in FAR_FIRST:
+        steps = FAR_FIRST
+        if kc < CHUNKS - 1:
+            far_slice = z_s.at[ring(z, 4, NZ), rows]
+            send(far_slice, z_q.at[rows], zz_send, zq_recv.at[kc], device(x, y, zm, core))
+            steps = (3, 2, 6, 1, 7)
+        for step in steps:
             zt = ring(z, step, NZ)
             send(z_s.at[zt, rows], z_r.at[step - 1, rows], zz_send,
                  zz_recv.at[kc], device(x, y, zt, core))
 
+    def relay_z(kc):
+        rows = rows_of(kc)
+        zt = ring(z, 5, NZ)
+        arrived(z_q.at[rows], zq_recv.at[kc])
+        z_s[zt, rows] = (z_s[zt, rows].astype(F32) + z_q[rows].astype(F32)).astype(BF16)
+        send(z_s.at[zt, rows], z_r.at[4, rows], zz_send, zz_recv.at[kc],
+             device(x, y, zt, core))
+
     def reduce_z(kc):
         rows = rows_of(kc)
-        arrived(z_r.at[:, rows], zz_recv.at[kc])
+        slots = (0, 1, 2, 4, 5, 6) if kc < CHUNKS - 1 else range(NZ - 1)
+        arrived(z_r.at[0:len(slots), rows], zz_recv.at[kc])
         total = z_s[z, rows].astype(F32)
-        for i in range(NZ - 1):
+        for i in slots:
             total = total + z_r[i, rows].astype(F32)
         g_full[core, rows] = total.astype(BF16)
         send(g_full.at[core, rows], g_full.at[core, rows], g_send, g_recv.at[kc],
@@ -351,14 +365,14 @@
         arrived(dga.at[0:2], dx_recv)
 
     M, B, S, C, Z = multiply, near_plain, near_sum, reduce_own, reduce_z
-    F, T = forward, send_tokens
+    D, F, T = relay_z, forward, send_tokens
     order = (
         (gathered, 0), (M, 0), (B, 0), (left_step, 3), (S, 0),
         (M, 1), (B, 1), (left_step, 4), (S, 1), (C, 0),
-        (F, 3), (T, 4), (M, 2), (B, 2), (S, 2), (C, 1), (Z, 0),
-        (F, 4), (right_send, 0), (M, 3), (B, 3), (S, 3), (C, 2), (Z, 1),
-        (M, 4), (B, 4), (S, 4), (C, 3), (Z, 2), (right_cross, 0),
-        (C, 4), (Z, 3), (left_most, 0), (Z, 4),
+        (F, 3), (T, 4), (M, 2), (B, 2), (S, 2), (D, 0), (C, 1),
+        (F, 4), (right_send, 0), (M, 3), (B, 3), (S, 3), (D, 1), (C, 2), (Z, 0),
+        (M, 4), (B, 4), (S, 4), (D, 2), (C, 3), (Z, 1), (right_cross, 0),
+        (Z, 2), (D, 3), (C, 4), (Z, 3), (left_most, 0), (Z, 4),
     )
     for step, kc in order:
         step(kc)
@@ -437,6 +451,7 @@
         vm((2, HALF, 1024), BF16),
         vm((NZ, HALF, 128), BF16),
         vm((NZ - 1, HALF, 128), BF16),
+        vm((HALF, 128), BF16),
         vm((2, HALF, 128), BF16),
         vm((4, 16, 1024), BF16),
         vm((NZ, 4, 16, 1024), BF16),
@@ -449,7 +464,7 @@
         dma, dma((CHUNKS,)), dma,
         dma((CHUNKS, 2)),
         dma, dma((CHUNKS, 2)), dma, dma((CHUNKS,)),
-        dma, dma((CHUNKS,)), dma, dma((CHUNKS,)),
+        dma, dma((CHUNKS,)), dma((CHUNKS,)), dma, dma((CHUNKS,)),
         dma, dma, dma, dma((NZ - 1,)), dma, dma((3,)),
         dma, dma((2,)), dma, dma, dma((6,)),
     ]

time: 94.9 us -> 97.6 us (1.028)
  Pallas kernels: 92.9 us -> 95.6 us
    pallas_call x1, Pallas kernels: 92.9 us -> 95.6 us  [local(): pl.pallas_call(kernel, out_shape=jax.ShapeDtypeStruct((2, 8, 16, 256), F3...]
where the time goes in v7:
time: 97.6 us; the launch traced here: 97.5 us
  Pallas kernels  95.6 us (98%)
  local copies, waits for them, and re-layouts  1.86 us (2%)
    pallas_call x1, Pallas kernels, local(): pl.pallas_call(kernel, out_shape=jax.ShapeDtypeStruct((2, 8, 16, 256), F3...  95.6 us

profile of v7, /device:TPU:1, one launch (start us, length us, event | category | flops | bytes accessed | tf_op | source)
XLA Modules:
  0.0 97.5 jit_solution(15497580739083843997)
XLA Ops:
  0.0 95.6 %shard_map.64 = f32[2,8,16,256]{3,2,1,0:T(8,128)} custom-call(bf16[128,8192]{1,0:T(8,128)(2,1)} %tok_hbm.1, bf16[512,256]{1,0:T(8,128)(2,1)} %gate_hbm.1, bf16[512,256]{1,0:T(8,128)(2,1)} %up_hbm.1, bf16[512,256]{1,0:T(8,128)(2,1)} %dh_hbm.1, bf16[16,8,2,1024]{3,2,1,0:T(2,128)(2,1)} %left_hbm.1, bf16[2,256,1024]{2,1,0:T(8,128)(2,1)} %right_hbm.1), custom_call_target="tpu_custom_call" | custom-call | flops 4499999744 | bytes 8000000 | tf_op jit(solution)/shard_map/pallas_call | solution.py:471
  95.6 1.9 %copy.7 = f32[16,8,2,256]{3,2,1,0:T(2,128)} copy(f32[16,8,2,256]{3,0,1,2:T(8,128)} %bitcast.1) | data formatting | bytes 524288 | tf_op jit(solution)/shard_map/transpose | solution.py:484

commit v8 on v6

--- a/solution.py
+++ b/solution.py
@@ -354,10 +354,10 @@
     F, T = forward, send_tokens
     order = (
         (gathered, 0), (M, 0), (B, 0), (left_step, 3), (S, 0),
-        (M, 1), (B, 1), (left_step, 4), (S, 1), (C, 0),
-        (F, 3), (T, 4), (M, 2), (B, 2), (S, 2), (C, 1), (Z, 0),
-        (F, 4), (right_send, 0), (M, 3), (B, 3), (S, 3), (C, 2), (Z, 1),
-        (M, 4), (B, 4), (S, 4), (C, 3), (Z, 2), (right_cross, 0),
+        (M, 1), (B, 1), (left_step, 4), (C, 0), (S, 1),
+        (F, 3), (T, 4), (M, 2), (B, 2), (C, 1), (S, 2), (Z, 0),
+        (F, 4), (right_send, 0), (M, 3), (B, 3), (C, 2), (S, 3), (Z, 1),
+        (M, 4), (B, 4), (C, 3), (S, 4), (Z, 2), (right_cross, 0),
         (C, 4), (Z, 3), (left_most, 0), (Z, 4),
     )
     for step, kc in order:

time: 94.9 us -> 94.2 us (level)
  no operation moved by 1% of the time
where the time goes in v8:
time: 94.2 us; the launch traced here: 94.1 us
  Pallas kernels  92.2 us (98%)
  local copies, waits for them, and re-layouts  1.86 us (2%)
    pallas_call x1, Pallas kernels, local(): pl.pallas_call(kernel, out_shape=jax.ShapeDtypeStruct((2, 8, 16, 256), F3...  92.2 us

profile of v8, /device:TPU:1, one launch (start us, length us, event | category | flops | bytes accessed | tf_op | source)
XLA Modules:
  0.0 94.1 jit_solution(15276091372736388104)
XLA Ops:
  0.0 92.2 %shard_map.64 = f32[2,8,16,256]{3,2,1,0:T(8,128)} custom-call(bf16[128,8192]{1,0:T(8,128)(2,1)} %tok_hbm.1, bf16[512,256]{1,0:T(8,128)(2,1)} %gate_hbm.1, bf16[512,256]{1,0:T(8,128)(2,1)} %up_hbm.1, bf16[512,256]{1,0:T(8,128)(2,1)} %dh_hbm.1, bf16[16,8,2,1024]{3,2,1,0:T(2,128)(2,1)} %left_hbm.1, bf16[2,256,1024]{2,1,0:T(8,128)(2,1)} %right_hbm.1), custom_call_target="tpu_custom_call" | custom-call | flops 4499999744 | bytes 8000000 | tf_op jit(solution)/shard_map/pallas_call | solution.py:456
  92.2 1.9 %copy.7 = f32[16,8,2,256]{3,2,1,0:T(2,128)} copy(f32[16,8,2,256]{3,0,1,2:T(8,128)} %bitcast.1) | data formatting | bytes 524288 | tf_op jit(solution)/shard_map/transpose | solution.py:469
